TPU v7x, 512 devices: a whole 4x4x16 slice. The times are simulated.
512 devices in a mesh: level: 8 (over x, core), row: 16 (over z), col: 4 (over y).
Axes of the slice: x: 4, y: 4, z: 16, core: 2. Of those that a mesh axis runs over, the one named last changes fastest.
Arguments:
- factor_tiles: bfloat16 [8, 64, 16, 4, 128, 128], P('level', 'row', None, 'col'), may hold values from -0.0625 to 0.0625
- tile_mask: int32 [8, 64, 16, 4], P('level', 'row', None, 'col'), may hold values from 0 to 1, as said below
- inverse_diagonal: bfloat16 [8, 16, 4, 128, 128], P('level', 'row', 'col'), may hold values from -1.5 to 1.5, as said below
- right_sides: float32 [8, 16, 4, 128, 128], P('level', 'row', 'col'), may hold values from -6 to 6
Outputs:
- forward_solution: bfloat16 [8, 16, 4, 128, 128], P('level', 'row', 'col')
- solution: bfloat16 [8, 16, 4, 128, 128], P('level', 'row', 'col')
Inputs may be any that keep to these rules, and one draw needn't show every extreme that they name: `tile_mask`: 1 where the factor holds the tile, 0 where it does not; tiles are present only where |i - j| <= 32 with j = q * 4 + c, a band that follows the elimination tree. `inverse_diagonal`: each 128 x 128 block is lower triangular, the inverse of a diagonal block of the factor.
All inputs are finite; a program needn't handle non-finite values.
Results may differ from a plain program's by a relative error of at most 0.035.
Values may be sent and summed in bfloat16 or wider, within the bound.
A program may use at most 64 MiB of HBM per device.

v0:
```python
import jax
import jax.numpy as jnp
from jax import lax
from jax.sharding import PartitionSpec as P


def shifted(block, axis, distance):
    devices = range(lax.axis_size(axis))
    route = [(i - distance, i) for i in devices if i - distance in devices]
    return lax.ppermute(block, axis, route)


def solve_block(inverse, values):
    return jnp.einsum(
        "kst,ktr->ksr", inverse, values.astype(jnp.bfloat16), preferred_element_type=jnp.float32
    ).astype(jnp.bfloat16)


def solve_transposed(inverse, values):
    return jnp.einsum(
        "kts,ktr->ksr", inverse, values.astype(jnp.bfloat16), preferred_element_type=jnp.float32
    ).astype(jnp.bfloat16)


def local(factor_tiles, tile_mask, inverse_diagonal, right_sides):
    nlev = lax.axis_size("level")
    ncol = lax.axis_size("col")
    masked = factor_tiles[0, :, :, 0] * tile_mask[0, :, :, 0][:, :, None, None].astype(jnp.bfloat16)
    block_rows = masked.shape[0]
    qcount = masked.shape[1]
    side = masked.shape[2]
    own_rows = block_rows // ncol
    masked_split = masked.reshape(own_rows, ncol, qcount, side, side)
    inverse = inverse_diagonal[0, :, 0]
    sides = right_sides[0, :, 0]
    total_cols = sides.shape[-1]
    width, count, split = (total_cols, nlev - 1, 0)
    solved = solve_block(inverse, sides)
    for step in range(1, count + 1):
        piece = solved
        arrived = shifted(piece, "level", 1)
        partial_value = jnp.einsum(
            "aqst,qtr->asr",
            masked,
            lax.all_gather(arrived, "row", axis=0, tiled=True),
            preferred_element_type=jnp.float32,
        )
        pieces = lax.all_to_all(
            partial_value.reshape(own_rows, ncol, side, width).astype(jnp.bfloat16),
            "col",
            split_axis=1,
            concat_axis=1,
            tiled=True,
        ).astype(jnp.float32)
        mine = jnp.sum(pieces, axis=1)
        source = sides
        solved = solve_block(inverse, source - mine)
    answer = solve_transposed(inverse, solved)
    for step in range(1, count + 1):
        piece = answer[:, None]
        fold_piece = lax.all_gather(piece, "col", axis=1, tiled=True)
        partial_value = jnp.einsum(
            "kcqst,kcsr->qtr", masked_split, fold_piece, preferred_element_type=jnp.float32
        )
        summed = lax.psum_scatter(
            partial_value.astype(jnp.bfloat16), "row", scatter_dimension=0, tiled=True
        ).astype(jnp.float32)
        arrived = shifted(summed.astype(jnp.bfloat16), "level", -1).astype(summed.dtype)
        source = solved.astype(jnp.float32)
        answer = solve_transposed(inverse, source - arrived)
    return (solved[None, :, None], answer[None, :, None])


def solution(mesh):
    placed = (
        P("level", "row", None, "col", None, None),
        P("level", "row", None, "col"),
        P("level", "row", "col", None, None),
        P("level", "row", "col", None, None),
    )
    return jax.shard_map(
        local,
        mesh=mesh,
        in_specs=placed,
        out_specs=(P("level", "row", "col", None, None), P("level", "row", "col", None, None)),
        check_vma=False,
    )
```

profile of v0, /device:TPU:1, one launch (start us, length us, event | category | flops | bytes accessed | tf_op | source)
XLA Modules:
  0.0 923.1 jit_solution(2617397229417016310)
XLA Ops:
  17.8 28.6 %all_gather.42 = bf16[16,128,128]{2,1,0:T(8,128)(2,1)S(1)} all-gather(bf16[1,128,128]{2,1,0:T(8,128)(2,1)S(1)} %collective-permute-done), channel_id=1, replica_groups=mesh['level'=8,'row'=16,'col'=4] {'row'}, dimensions={0}, use_global_device_ids=true | all-gather | bytes 557056 | tf_op jit(solution)/shard_map/all_gather | solution.py:45
  57.9 12.0 %collective-permute-start.1 = (bf16[1,128,128]{1,2,0:T(8,128)(2,1)S(1)}, bf16[1,128,128]{1,2,0:T(8,128)(2,1)S(1)}, u32[]{:S(2)}, u32[]{:S(2)}) collective-permute-start(bf16[1,128,128]{1,2,0:T(8,128)(2,1)S(1)} %fusion.71), channel_id=1, source_target_pairs={{0,64},{64,128},{128,192},{192,256},{256,320},{320,384},{384,448},... | collective-permute-start | bytes 98312 | tf_op jit(solution)/shard_map/ppermute | solution.py:10
  71.0 22.7 %all_gather.43 = bf16[16,128,128]{2,1,0:T(8,128)(2,1)S(1)} all-gather(bf16[1,128,128]{2,1,0:T(8,128)(2,1)S(1)} %copy.36), channel_id=1, replica_groups=mesh['level'=8,'row'=16,'col'=4] {'row'}, dimensions={0}, use_global_device_ids=true | all-gather | bytes 557056 | tf_op jit(solution)/shard_map/all_gather | solution.py:45
  101.9 12.0 %collective-permute-start.2 = (bf16[1,128,128]{1,2,0:T(8,128)(2,1)S(1)}, bf16[1,128,128]{1,2,0:T(8,128)(2,1)S(1)}, u32[]{:S(2)}, u32[]{:S(2)}) collective-permute-start(bf16[1,128,128]{1,2,0:T(8,128)(2,1)S(1)} %fusion.72), channel_id=1, source_target_pairs={{0,64},{64,128},{128,192},{192,256},{256,320},{320,384},{384,448},... | collective-permute-start | bytes 98312 | tf_op jit(solution)/shard_map/ppermute | solution.py:10
  115.0 23.8 %all_gather.44 = bf16[16,128,128]{2,1,0:T(8,128)(2,1)S(1)} all-gather(bf16[1,128,128]{2,1,0:T(8,128)(2,1)S(1)} %copy.38), channel_id=1, replica_groups=mesh['level'=8,'row'=16,'col'=4] {'row'}, dimensions={0}, use_global_device_ids=true | all-gather | bytes 557056 | tf_op jit(solution)/shard_map/all_gather | solution.py:45
  147.9 11.6 %collective-permute-start.3 = (bf16[1,128,128]{1,2,0:T(8,128)(2,1)S(1)}, bf16[1,128,128]{1,2,0:T(8,128)(2,1)S(1)}, u32[]{:S(2)}, u32[]{:S(2)}) collective-permute-start(bf16[1,128,128]{1,2,0:T(8,128)(2,1)S(1)} %fusion.73), channel_id=1, source_target_pairs={{0,64},{64,128},{128,192},{192,256},{256,320},{320,384},{384,448},... | collective-permute-start | bytes 98312 | tf_op jit(solution)/shard_map/ppermute | solution.py:10
  160.7 22.7 %all_gather.45 = bf16[16,128,128]{2,1,0:T(8,128)(2,1)S(1)} all-gather(bf16[1,128,128]{2,1,0:T(8,128)(2,1)S(1)} %copy.40), channel_id=1, replica_groups=mesh['level'=8,'row'=16,'col'=4] {'row'}, dimensions={0}, use_global_device_ids=true | all-gather | bytes 557056 | tf_op jit(solution)/shard_map/all_gather | solution.py:45
  191.6 11.7 %collective-permute-start.4 = (bf16[1,128,128]{1,2,0:T(8,128)(2,1)S(1)}, bf16[1,128,128]{1,2,0:T(8,128)(2,1)S(1)}, u32[]{:S(2)}, u32[]{:S(2)}) collective-permute-start(bf16[1,128,128]{1,2,0:T(8,128)(2,1)S(1)} %fusion.74), channel_id=1, source_target_pairs={{0,64},{64,128},{128,192},{192,256},{256,320},{320,384},{384,448},... | collective-permute-start | bytes 98312 | tf_op jit(solution)/shard_map/ppermute | solution.py:10
  204.4 23.7 %all_gather.46 = bf16[16,128,128]{2,1,0:T(8,128)(2,1)S(1)} all-gather(bf16[1,128,128]{2,1,0:T(8,128)(2,1)S(1)} %copy.42), channel_id=1, replica_groups=mesh['level'=8,'row'=16,'col'=4] {'row'}, dimensions={0}, use_global_device_ids=true | all-gather | bytes 557056 | tf_op jit(solution)/shard_map/all_gather | solution.py:45
  236.2 12.5 %collective-permute-start.5 = (bf16[1,128,128]{1,2,0:T(8,128)(2,1)S(1)}, bf16[1,128,128]{1,2,0:T(8,128)(2,1)S(1)}, u32[]{:S(2)}, u32[]{:S(2)}) collective-permute-start(bf16[1,128,128]{1,2,0:T(8,128)(2,1)S(1)} %fusion.75), channel_id=1, source_target_pairs={{0,64},{64,128},{128,192},{192,256},{256,320},{320,384},{384,448},... | collective-permute-start | bytes 98312 | tf_op jit(solution)/shard_map/ppermute | solution.py:10
  249.8 22.7 %all_gather.47 = bf16[16,128,128]{2,1,0:T(8,128)(2,1)S(1)} all-gather(bf16[1,128,128]{2,1,0:T(8,128)(2,1)S(1)} %copy.44), channel_id=1, replica_groups=mesh['level'=8,'row'=16,'col'=4] {'row'}, dimensions={0}, use_global_device_ids=true | all-gather | bytes 557056 | tf_op jit(solution)/shard_map/all_gather | solution.py:45
  280.8 12.4 %collective-permute-start.6 = (bf16[1,128,128]{1,2,0:T(8,128)(2,1)S(1)}, bf16[1,128,128]{1,2,0:T(8,128)(2,1)S(1)}, u32[]{:S(2)}, u32[]{:S(2)}) collective-permute-start(bf16[1,128,128]{1,2,0:T(8,128)(2,1)S(1)} %fusion.76), channel_id=1, source_target_pairs={{0,64},{64,128},{128,192},{192,256},{256,320},{320,384},{384,448},... | collective-permute-start | bytes 98312 | tf_op jit(solution)/shard_map/ppermute | solution.py:10
  294.2 23.5 %all_gather.48 = bf16[16,128,128]{2,1,0:T(8,128)(2,1)S(1)} all-gather(bf16[1,128,128]{2,1,0:T(8,128)(2,1)S(1)} %copy.46), channel_id=1, replica_groups=mesh['level'=8,'row'=16,'col'=4] {'row'}, dimensions={0}, use_global_device_ids=true | all-gather | bytes 557056 | tf_op jit(solution)/shard_map/all_gather | solution.py:45
  336.1 64.7 %reduce-scatter.8.cloned.1.call-done = bf16[1,128,128]{1,2,0:T(8,128)(2,1)} async-done(((bf16[16,128,128]{1,2,0:T(8,128)(2,1)}), bf16[1,128,128]{1,2,0:T(8,128)(2,1)}) %reduce-scatter.8.cloned.1.call-update) | async-done | bytes 32784 | tf_op jit(solution)/shard_map/reduce_scatter | solution.py:65
  400.8 13.2 %collective-permute-start.7 = (bf16[1,128,128]{1,2,0:T(8,128)(2,1)}, bf16[1,128,128]{1,2,0:T(8,128)(2,1)S(1)}, u32[]{:S(2)}, u32[]{:S(2)}) collective-permute-start(bf16[1,128,128]{1,2,0:T(8,128)(2,1)} %reduce-scatter.8.cloned.1.call-done), channel_id=1, source_target_pairs={{64,0},{128,64},{192,128},{256,192},{320,256},{384,320},{448,384},... | collective-permute-start | bytes 98312 | tf_op jit(solution)/shard_map/ppermute | solution.py:10
  427.9 55.9 %reduce-scatter.10.cloned.1.call-done = bf16[1,128,128]{1,2,0:T(8,128)(2,1)} async-done(((bf16[16,128,128]{1,2,0:T(8,128)(2,1)}), bf16[1,128,128]{1,2,0:T(8,128)(2,1)}) %reduce-scatter.10.cloned.1.call-update) | async-done | bytes 32784 | tf_op jit(solution)/shard_map/reduce_scatter | solution.py:65
  483.8 13.3 %collective-permute-start.8 = (bf16[1,128,128]{1,2,0:T(8,128)(2,1)}, bf16[1,128,128]{1,2,0:T(8,128)(2,1)S(1)}, u32[]{:S(2)}, u32[]{:S(2)}) collective-permute-start(bf16[1,128,128]{1,2,0:T(8,128)(2,1)} %reduce-scatter.10.cloned.1.call-done), channel_id=1, source_target_pairs={{64,0},{128,64},{192,128},{256,192},{320,256},{384,320},{448,384},... | collective-permute-start | bytes 98312 | tf_op jit(solution)/shard_map/ppermute | solution.py:10
  500.0 9.4 %all-gather.2 = bf16[512,128]{0,1:T(8,128)(2,1)S(1)} all-gather(bf16[128,128]{0,1:T(8,128)(2,1)S(1)} %fusion.79), channel_id=4, replica_groups=mesh['level'=8,'row'=16,'col'=4] {'col'}, dimensions={0}, use_global_device_ids=true | all-gather | bytes 163840 | tf_op jit(solution)/shard_map/all_gather | solution.py:61
  511.0 55.9 %reduce-scatter.12.cloned.1.call-done = bf16[1,128,128]{1,2,0:T(8,128)(2,1)} async-done(((bf16[16,128,128]{1,2,0:T(8,128)(2,1)}), bf16[1,128,128]{1,2,0:T(8,128)(2,1)}) %reduce-scatter.12.cloned.1.call-update) | async-done | bytes 32784 | tf_op jit(solution)/shard_map/reduce_scatter | solution.py:65
  566.9 13.2 %collective-permute-start.9 = (bf16[1,128,128]{1,2,0:T(8,128)(2,1)}, bf16[1,128,128]{1,2,0:T(8,128)(2,1)S(1)}, u32[]{:S(2)}, u32[]{:S(2)}) collective-permute-start(bf16[1,128,128]{1,2,0:T(8,128)(2,1)} %reduce-scatter.12.cloned.1.call-done), channel_id=1, source_target_pairs={{64,0},{128,64},{192,128},{256,192},{320,256},{384,320},{448,384},... | collective-permute-start | bytes 98312 | tf_op jit(solution)/shard_map/ppermute | solution.py:10
  583.1 9.4 %all-gather.3 = bf16[512,128]{0,1:T(8,128)(2,1)S(1)} all-gather(bf16[128,128]{0,1:T(8,128)(2,1)S(1)} %fusion.80), channel_id=5, replica_groups=mesh['level'=8,'row'=16,'col'=4] {'col'}, dimensions={0}, use_global_device_ids=true | all-gather | bytes 163840 | tf_op jit(solution)/shard_map/all_gather | solution.py:61
  594.1 55.3 %reduce-scatter.14.cloned.1.call-done = bf16[1,128,128]{1,2,0:T(8,128)(2,1)} async-done(((bf16[16,128,128]{1,2,0:T(8,128)(2,1)}), bf16[1,128,128]{1,2,0:T(8,128)(2,1)}) %reduce-scatter.14.cloned.1.call-update) | async-done | bytes 32784 | tf_op jit(solution)/shard_map/reduce_scatter | solution.py:65
  649.4 13.9 %collective-permute-start.10 = (bf16[1,128,128]{1,2,0:T(8,128)(2,1)}, bf16[1,128,128]{1,2,0:T(8,128)(2,1)S(1)}, u32[]{:S(2)}, u32[]{:S(2)}) collective-permute-start(bf16[1,128,128]{1,2,0:T(8,128)(2,1)} %reduce-scatter.14.cloned.1.call-done), channel_id=1, source_target_pairs={{64,0},{128,64},{192,128},{256,192},{320,256},{384,320},{448,384},... | collective-permute-start | bytes 98312 | tf_op jit(solution)/shard_map/ppermute | solution.py:10
  666.2 9.5 %all-gather.4 = bf16[512,128]{0,1:T(8,128)(2,1)S(1)} all-gather(bf16[128,128]{0,1:T(8,128)(2,1)S(1)} %fusion.81), channel_id=6, replica_groups=mesh['level'=8,'row'=16,'col'=4] {'col'}, dimensions={0}, use_global_device_ids=true | all-gather | bytes 163840 | tf_op jit(solution)/shard_map/all_gather | solution.py:61
  677.2 55.5 %reduce-scatter.16.cloned.1.call-done = bf16[1,128,128]{1,2,0:T(8,128)(2,1)} async-done(((bf16[16,128,128]{1,2,0:T(8,128)(2,1)}), bf16[1,128,128]{1,2,0:T(8,128)(2,1)}) %reduce-scatter.16.cloned.1.call-update) | async-done | bytes 32784 | tf_op jit(solution)/shard_map/reduce_scatter | solution.py:65
  732.8 13.6 %collective-permute-start.11 = (bf16[1,128,128]{1,2,0:T(8,128)(2,1)}, bf16[1,128,128]{1,2,0:T(8,128)(2,1)S(1)}, u32[]{:S(2)}, u32[]{:S(2)}) collective-permute-start(bf16[1,128,128]{1,2,0:T(8,128)(2,1)} %reduce-scatter.16.cloned.1.call-done), channel_id=1, source_target_pairs={{64,0},{128,64},{192,128},{256,192},{320,256},{384,320},{448,384},... | collective-permute-start | bytes 98312 | tf_op jit(solution)/shard_map/ppermute | solution.py:10
  749.4 9.5 %all-gather.5 = bf16[512,128]{0,1:T(8,128)(2,1)S(1)} all-gather(bf16[128,128]{0,1:T(8,128)(2,1)S(1)} %fusion.82), channel_id=7, replica_groups=mesh['level'=8,'row'=16,'col'=4] {'col'}, dimensions={0}, use_global_device_ids=true | all-gather | bytes 163840 | tf_op jit(solution)/shard_map/all_gather | solution.py:61
  760.4 55.8 %reduce-scatter.18.cloned.1.call-done = bf16[1,128,128]{1,2,0:T(8,128)(2,1)} async-done(((bf16[16,128,128]{1,2,0:T(8,128)(2,1)}), bf16[1,128,128]{1,2,0:T(8,128)(2,1)}) %reduce-scatter.18.cloned.1.call-update) | async-done | bytes 32784 | tf_op jit(solution)/shard_map/reduce_scatter | solution.py:65
  816.2 13.2 %collective-permute-start.12 = (bf16[1,128,128]{1,2,0:T(8,128)(2,1)}, bf16[1,128,128]{1,2,0:T(8,128)(2,1)S(1)}, u32[]{:S(2)}, u32[]{:S(2)}) collective-permute-start(bf16[1,128,128]{1,2,0:T(8,128)(2,1)} %reduce-scatter.18.cloned.1.call-done), channel_id=1, source_target_pairs={{64,0},{128,64},{192,128},{256,192},{320,256},{384,320},{448,384},... | collective-permute-start | bytes 98312 | tf_op jit(solution)/shard_map/ppermute | solution.py:10
  832.4 9.5 %all-gather.6 = bf16[512,128]{0,1:T(8,128)(2,1)S(1)} all-gather(bf16[128,128]{0,1:T(8,128)(2,1)S(1)} %fusion.83), channel_id=8, replica_groups=mesh['level'=8,'row'=16,'col'=4] {'col'}, dimensions={0}, use_global_device_ids=true | all-gather | bytes 163840 | tf_op jit(solution)/shard_map/all_gather | solution.py:61
  843.4 55.8 %reduce-scatter.20.cloned.1.call-done = bf16[1,128,128]{1,2,0:T(8,128)(2,1)} async-done(((bf16[16,128,128]{1,2,0:T(8,128)(2,1)}), bf16[1,128,128]{1,2,0:T(8,128)(2,1)}) %reduce-scatter.20.cloned.1.call-update) | async-done | bytes 32784 | tf_op jit(solution)/shard_map/reduce_scatter | solution.py:65
  899.2 13.2 %collective-permute-start.13 = (bf16[1,128,128]{1,2,0:T(8,128)(2,1)}, bf16[1,128,128]{1,2,0:T(8,128)(2,1)S(1)}, u32[]{:S(2)}, u32[]{:S(2)}) collective-permute-start(bf16[1,128,128]{1,2,0:T(8,128)(2,1)} %reduce-scatter.20.cloned.1.call-done), channel_id=1, source_target_pairs={{64,0},{128,64},{192,128},{256,192},{320,256},{384,320},{448,384},... | collective-permute-start | bytes 98312 | tf_op jit(solution)/shard_map/ppermute | solution.py:10
  (98 shorter events, 128.9 us)
Async XLA Ops:
  7.2 0.8 copy-start
  7.2 393.6 %reduce-scatter.8.cloned.1.call-start = ((), (), s32[]{:S(2)}) async-start(), calls=%async_computation.14 | async-start | bytes 557056 | tf_op jit(solution)/shard_map/reduce_scatter | solution.py:65
  8.9 8.9 collective-permute-start
  46.3 11.3 %copy-start.1 = (f32[1,1,1,128,128]{4,3,2,1,0:T(8,128)S(1)}, f32[1,1,1,128,128]{4,3,2,1,0:T(8,128)}, u32[]{:S(2)}) copy-start(f32[1,1,1,128,128]{4,3,2,1,0:T(8,128)} %param.7) | copy-start | bytes 196612
  46.3 47.4 %copy-start.2 = (bf16[1,4,16,1,128,128]{5,4,3,2,1,0:T(8,128)(2,1)S(1)}, bf16[1,4,16,1,128,128]{5,4,3,2,1,0:T(8,128)(2,1)}, u32[]{:S(2)}) copy-start(bf16[1,4,16,1,128,128]{5,4,3,2,1,0:T(8,128)(2,1)} %param.4) | copy-start | bytes 6291460
  57.9 13.0 %collective-permute-start.1 = (bf16[1,128,128]{1,2,0:T(8,128)(2,1)S(1)}, bf16[1,128,128]{1,2,0:T(8,128)(2,1)S(1)}, u32[]{:S(2)}, u32[]{:S(2)}) collective-permute-start(bf16[1,128,128]{1,2,0:T(8,128)(2,1)S(1)} %fusion.71), channel_id=1, source_target_pairs={{0,64},{64,128},{128,192},{192,256},{256,320},{320,384},{384,448},... | collective-permute-start | bytes 98312 | tf_op jit(solution)/shard_map/ppermute | solution.py:10
  101.9 13.0 %collective-permute-start.2 = (bf16[1,128,128]{1,2,0:T(8,128)(2,1)S(1)}, bf16[1,128,128]{1,2,0:T(8,128)(2,1)S(1)}, u32[]{:S(2)}, u32[]{:S(2)}) collective-permute-start(bf16[1,128,128]{1,2,0:T(8,128)(2,1)S(1)} %fusion.72), channel_id=1, source_target_pairs={{0,64},{64,128},{128,192},{192,256},{256,320},{320,384},{384,448},... | collective-permute-start | bytes 98312 | tf_op jit(solution)/shard_map/ppermute | solution.py:10
  147.9 12.6 %collective-permute-start.3 = (bf16[1,128,128]{1,2,0:T(8,128)(2,1)S(1)}, bf16[1,128,128]{1,2,0:T(8,128)(2,1)S(1)}, u32[]{:S(2)}, u32[]{:S(2)}) collective-permute-start(bf16[1,128,128]{1,2,0:T(8,128)(2,1)S(1)} %fusion.73), channel_id=1, source_target_pairs={{0,64},{64,128},{128,192},{192,256},{256,320},{320,384},{384,448},... | collective-permute-start | bytes 98312 | tf_op jit(solution)/shard_map/ppermute | solution.py:10
  191.6 12.7 %collective-permute-start.4 = (bf16[1,128,128]{1,2,0:T(8,128)(2,1)S(1)}, bf16[1,128,128]{1,2,0:T(8,128)(2,1)S(1)}, u32[]{:S(2)}, u32[]{:S(2)}) collective-permute-start(bf16[1,128,128]{1,2,0:T(8,128)(2,1)S(1)} %fusion.74), channel_id=1, source_target_pairs={{0,64},{64,128},{128,192},{192,256},{256,320},{320,384},{384,448},... | collective-permute-start | bytes 98312 | tf_op jit(solution)/shard_map/ppermute | solution.py:10
  236.2 13.5 %collective-permute-start.5 = (bf16[1,128,128]{1,2,0:T(8,128)(2,1)S(1)}, bf16[1,128,128]{1,2,0:T(8,128)(2,1)S(1)}, u32[]{:S(2)}, u32[]{:S(2)}) collective-permute-start(bf16[1,128,128]{1,2,0:T(8,128)(2,1)S(1)} %fusion.75), channel_id=1, source_target_pairs={{0,64},{64,128},{128,192},{192,256},{256,320},{320,384},{384,448},... | collective-permute-start | bytes 98312 | tf_op jit(solution)/shard_map/ppermute | solution.py:10
  280.8 13.4 %collective-permute-start.6 = (bf16[1,128,128]{1,2,0:T(8,128)(2,1)S(1)}, bf16[1,128,128]{1,2,0:T(8,128)(2,1)S(1)}, u32[]{:S(2)}, u32[]{:S(2)}) collective-permute-start(bf16[1,128,128]{1,2,0:T(8,128)(2,1)S(1)} %fusion.76), channel_id=1, source_target_pairs={{0,64},{64,128},{128,192},{192,256},{256,320},{320,384},{384,448},... | collective-permute-start | bytes 98312 | tf_op jit(solution)/shard_map/ppermute | solution.py:10
  336.0 147.8 %reduce-scatter.10.cloned.1.call-start = ((), (), s32[]{:S(2)}) async-start(), calls=%async_computation.15 | async-start | bytes 557056 | tf_op jit(solution)/shard_map/reduce_scatter | solution.py:65
  400.8 16.1 %collective-permute-start.7 = (bf16[1,128,128]{1,2,0:T(8,128)(2,1)}, bf16[1,128,128]{1,2,0:T(8,128)(2,1)S(1)}, u32[]{:S(2)}, u32[]{:S(2)}) collective-permute-start(bf16[1,128,128]{1,2,0:T(8,128)(2,1)} %reduce-scatter.8.cloned.1.call-done), channel_id=1, source_target_pairs={{64,0},{128,64},{192,128},{256,192},{320,256},{384,320},{448,384},... | collective-permute-start | bytes 98312 | tf_op jit(solution)/shard_map/ppermute | solution.py:10
  427.9 139.0 %reduce-scatter.12.cloned.1.call-start = ((), (), s32[]{:S(2)}) async-start(), calls=%async_computation.16 | async-start | bytes 557056 | tf_op jit(solution)/shard_map/reduce_scatter | solution.py:65
  483.8 16.1 %collective-permute-start.8 = (bf16[1,128,128]{1,2,0:T(8,128)(2,1)}, bf16[1,128,128]{1,2,0:T(8,128)(2,1)S(1)}, u32[]{:S(2)}, u32[]{:S(2)}) collective-permute-start(bf16[1,128,128]{1,2,0:T(8,128)(2,1)} %reduce-scatter.10.cloned.1.call-done), channel_id=1, source_target_pairs={{64,0},{128,64},{192,128},{256,192},{320,256},{384,320},{448,384},... | collective-permute-start | bytes 98312 | tf_op jit(solution)/shard_map/ppermute | solution.py:10
  510.9 138.5 %reduce-scatter.14.cloned.1.call-start = ((), (), s32[]{:S(2)}) async-start(), calls=%async_computation.17 | async-start | bytes 557056 | tf_op jit(solution)/shard_map/reduce_scatter | solution.py:65
  566.9 16.1 %collective-permute-start.9 = (bf16[1,128,128]{1,2,0:T(8,128)(2,1)}, bf16[1,128,128]{1,2,0:T(8,128)(2,1)S(1)}, u32[]{:S(2)}, u32[]{:S(2)}) collective-permute-start(bf16[1,128,128]{1,2,0:T(8,128)(2,1)} %reduce-scatter.12.cloned.1.call-done), channel_id=1, source_target_pairs={{64,0},{128,64},{192,128},{256,192},{320,256},{384,320},{448,384},... | collective-permute-start | bytes 98312 | tf_op jit(solution)/shard_map/ppermute | solution.py:10
  594.0 138.7 %reduce-scatter.16.cloned.1.call-start = ((), (), s32[]{:S(2)}) async-start(), calls=%async_computation.18 | async-start | bytes 557056 | tf_op jit(solution)/shard_map/reduce_scatter | solution.py:65
  649.4 16.7 %collective-permute-start.10 = (bf16[1,128,128]{1,2,0:T(8,128)(2,1)}, bf16[1,128,128]{1,2,0:T(8,128)(2,1)S(1)}, u32[]{:S(2)}, u32[]{:S(2)}) collective-permute-start(bf16[1,128,128]{1,2,0:T(8,128)(2,1)} %reduce-scatter.14.cloned.1.call-done), channel_id=1, source_target_pairs={{64,0},{128,64},{192,128},{256,192},{320,256},{384,320},{448,384},... | collective-permute-start | bytes 98312 | tf_op jit(solution)/shard_map/ppermute | solution.py:10
  677.2 139.0 %reduce-scatter.18.cloned.1.call-start = ((), (), s32[]{:S(2)}) async-start(), calls=%async_computation.19 | async-start | bytes 557056 | tf_op jit(solution)/shard_map/reduce_scatter | solution.py:65
  732.8 16.5 %collective-permute-start.11 = (bf16[1,128,128]{1,2,0:T(8,128)(2,1)}, bf16[1,128,128]{1,2,0:T(8,128)(2,1)S(1)}, u32[]{:S(2)}, u32[]{:S(2)}) collective-permute-start(bf16[1,128,128]{1,2,0:T(8,128)(2,1)} %reduce-scatter.16.cloned.1.call-done), channel_id=1, source_target_pairs={{64,0},{128,64},{192,128},{256,192},{320,256},{384,320},{448,384},... | collective-permute-start | bytes 98312 | tf_op jit(solution)/shard_map/ppermute | solution.py:10
  760.4 138.8 %reduce-scatter.20.cloned.1.call-start = ((), (), s32[]{:S(2)}) async-start(), calls=%async_computation.20 | async-start | bytes 557056 | tf_op jit(solution)/shard_map/reduce_scatter | solution.py:65
  816.2 16.1 %collective-permute-start.12 = (bf16[1,128,128]{1,2,0:T(8,128)(2,1)}, bf16[1,128,128]{1,2,0:T(8,128)(2,1)S(1)}, u32[]{:S(2)}, u32[]{:S(2)}) collective-permute-start(bf16[1,128,128]{1,2,0:T(8,128)(2,1)} %reduce-scatter.18.cloned.1.call-done), channel_id=1, source_target_pairs={{64,0},{128,64},{192,128},{256,192},{320,256},{384,320},{448,384},... | collective-permute-start | bytes 98312 | tf_op jit(solution)/shard_map/ppermute | solution.py:10
  899.2 16.2 %collective-permute-start.13 = (bf16[1,128,128]{1,2,0:T(8,128)(2,1)}, bf16[1,128,128]{1,2,0:T(8,128)(2,1)S(1)}, u32[]{:S(2)}, u32[]{:S(2)}) collective-permute-start(bf16[1,128,128]{1,2,0:T(8,128)(2,1)} %reduce-scatter.20.cloned.1.call-done), channel_id=1, source_target_pairs={{64,0},{128,64},{192,128},{256,192},{320,256},{384,320},{448,384},... | collective-permute-start | bytes 98312 | tf_op jit(solution)/shard_map/ppermute | solution.py:10
Sparse Core Ops, SparseCore 0:
  336.1 64.5 reduce-scatter.7
  428.0 55.7 reduce-scatter.9
  511.0 55.7 reduce-scatter.11
  594.1 55.2 reduce-scatter.13
  677.3 55.4 reduce-scatter.15
  760.5 55.6 reduce-scatter.17
  843.5 55.6 reduce-scatter.19
where the time goes:
time: 924 us; the launch traced here: 923 us
  waiting for transfers between devices  428 us (46%)
  blocking collectives  286 us (31%)
  starting transfers between devices  170 us (18%)
  matrix products  19.6 us (2%)
  between operations  14.5 us (2%)
    reduce_scatter x7, waiting for transfers between devices, local(): lax.psum_scatter(partial_value.astype(jnp.bfloat16), 'row', scatter_dimen...  399 us
    ppermute x14, starting transfers between devices, shifted(): return lax.ppermute(block, axis, route)  170 us
    all_gather x7, blocking collectives, local(): lax.all_gather(arrived, 'row', axis=0, tiled=True)  168 us
    all_gather x7, blocking collectives, local(): fold_piece = lax.all_gather(piece, 'col', axis=1, tiled=True)  65.2 us
    all_to_all x7, blocking collectives, local(): lax.all_to_all(partial_value.reshape(own_rows, ncol, side, width).astype(...  53 us
    ppermute x14, waiting for transfers between devices, shifted(): return lax.ppermute(block, axis, route)  29.1 us
  transfers between devices with their start and end apart: 21, of which 21 were waited for; matrix products, arithmetic and copies ran while one was open for 0% of the time, Pallas kernels for 0%

commit v1 on v0

--- a/solution.py
+++ b/solution.py
@@ -58,7 +58,9 @@
     answer = solve_transposed(inverse, solved)
     for step in range(1, count + 1):
         piece = answer[:, None]
-        fold_piece = lax.all_gather(piece, "col", axis=1, tiled=True)
+        fold_piece = jnp.concatenate(
+            lax.all_to_all(jnp.stack([piece] * lax.axis_size("col")), "col", 0, 0), axis=1
+        )
         partial_value = jnp.einsum(
             "kcqst,kcsr->qtr", masked_split, fold_piece, preferred_element_type=jnp.float32
         )

time: 924 us -> 910 us (0.985)
  waiting for transfers between devices: 428 us -> 418 us
    all_gather x7 -> x0, blocking collectives: 65.2 us -> none  [local(): fold_piece = lax.all_gather(piece, 'col', axis=1, tiled=True)]
    all_to_all x0 -> x7, blocking collectives: none -> 59.2 us  [local(): lax.all_to_all(jnp.stack([piece] * lax.axis_size('col')), 'col', 0, 0)]
    reduce_scatter x7, waiting for transfers between devices: 399 us -> 389 us  [local(): lax.psum_scatter(partial_value.astype(jnp.bfloat16), 'row', scatter_dimen...]
where the time goes in v1:
time: 910 us; the launch traced here: 909 us
  waiting for transfers between devices  418 us (46%)
  blocking collectives  280 us (31%)
  starting transfers between devices  172 us (19%)
  matrix products  19.5 us (2%)
  between operations  14.5 us (2%)
    reduce_scatter x7, waiting for transfers between devices, local(): lax.psum_scatter(partial_value.astype(jnp.bfloat16), 'row', scatter_dimen...  389 us
    ppermute x14, starting transfers between devices, shifted(): return lax.ppermute(block, axis, route)  172 us
    all_gather x7, blocking collectives, local(): lax.all_gather(arrived, 'row', axis=0, tiled=True)  168 us
    all_to_all x7, blocking collectives, local(): lax.all_to_all(jnp.stack([piece] * lax.axis_size('col')), 'col', 0, 0)  59.2 us
    all_to_all x7, blocking collectives, local(): lax.all_to_all(partial_value.reshape(own_rows, ncol, side, width).astype(...  53 us
    ppermute x14, waiting for transfers between devices, shifted(): return lax.ppermute(block, axis, route)  28.8 us
  transfers between devices with their start and end apart: 21, of which 21 were waited for; matrix products, arithmetic and copies ran while one was open for 0% of the time, Pallas kernels for 0%

profile of v1, /device:TPU:1, one launch (start us, length us, event | category | flops | bytes accessed | tf_op | source)
XLA Modules:
  0.0 908.5 jit_solution(8010556495176849007)
XLA Ops:
  17.8 28.6 %all_gather.21 = bf16[16,128,128]{2,1,0:T(8,128)(2,1)S(1)} all-gather(bf16[1,128,128]{2,1,0:T(8,128)(2,1)S(1)} %collective-permute-done), channel_id=1, replica_groups=mesh['level'=8,'row'=16,'col'=4] {'row'}, dimensions={0}, use_global_device_ids=true | all-gather | bytes 557056 | tf_op jit(solution)/shard_map/all_gather | solution.py:45
  48.8 8.8 all_to_all.70
  57.9 12.0 %collective-permute-start.1 = (bf16[1,128,128]{1,2,0:T(8,128)(2,1)S(1)}, bf16[1,128,128]{1,2,0:T(8,128)(2,1)S(1)}, u32[]{:S(2)}, u32[]{:S(2)}) collective-permute-start(bf16[1,128,128]{1,2,0:T(8,128)(2,1)S(1)} %fusion.71), channel_id=1, source_target_pairs={{0,64},{64,128},{128,192},{192,256},{256,320},{320,384},{384,448},... | collective-permute-start | bytes 98312 | tf_op jit(solution)/shard_map/ppermute | solution.py:10
  71.0 22.7 %all_gather.22 = bf16[16,128,128]{2,1,0:T(8,128)(2,1)S(1)} all-gather(bf16[1,128,128]{2,1,0:T(8,128)(2,1)S(1)} %copy.36), channel_id=1, replica_groups=mesh['level'=8,'row'=16,'col'=4] {'row'}, dimensions={0}, use_global_device_ids=true | all-gather | bytes 557056 | tf_op jit(solution)/shard_map/all_gather | solution.py:45
  101.9 12.0 %collective-permute-start.2 = (bf16[1,128,128]{1,2,0:T(8,128)(2,1)S(1)}, bf16[1,128,128]{1,2,0:T(8,128)(2,1)S(1)}, u32[]{:S(2)}, u32[]{:S(2)}) collective-permute-start(bf16[1,128,128]{1,2,0:T(8,128)(2,1)S(1)} %fusion.72), channel_id=1, source_target_pairs={{0,64},{64,128},{128,192},{192,256},{256,320},{320,384},{384,448},... | collective-permute-start | bytes 98312 | tf_op jit(solution)/shard_map/ppermute | solution.py:10
  115.0 23.8 %all_gather.23 = bf16[16,128,128]{2,1,0:T(8,128)(2,1)S(1)} all-gather(bf16[1,128,128]{2,1,0:T(8,128)(2,1)S(1)} %copy.38), channel_id=1, replica_groups=mesh['level'=8,'row'=16,'col'=4] {'row'}, dimensions={0}, use_global_device_ids=true | all-gather | bytes 557056 | tf_op jit(solution)/shard_map/all_gather | solution.py:45
  147.9 11.6 %collective-permute-start.3 = (bf16[1,128,128]{1,2,0:T(8,128)(2,1)S(1)}, bf16[1,128,128]{1,2,0:T(8,128)(2,1)S(1)}, u32[]{:S(2)}, u32[]{:S(2)}) collective-permute-start(bf16[1,128,128]{1,2,0:T(8,128)(2,1)S(1)} %fusion.73), channel_id=1, source_target_pairs={{0,64},{64,128},{128,192},{192,256},{256,320},{320,384},{384,448},... | collective-permute-start | bytes 98312 | tf_op jit(solution)/shard_map/ppermute | solution.py:10
  160.7 22.7 %all_gather.24 = bf16[16,128,128]{2,1,0:T(8,128)(2,1)S(1)} all-gather(bf16[1,128,128]{2,1,0:T(8,128)(2,1)S(1)} %copy.40), channel_id=1, replica_groups=mesh['level'=8,'row'=16,'col'=4] {'row'}, dimensions={0}, use_global_device_ids=true | all-gather | bytes 557056 | tf_op jit(solution)/shard_map/all_gather | solution.py:45
  191.6 11.7 %collective-permute-start.4 = (bf16[1,128,128]{1,2,0:T(8,128)(2,1)S(1)}, bf16[1,128,128]{1,2,0:T(8,128)(2,1)S(1)}, u32[]{:S(2)}, u32[]{:S(2)}) collective-permute-start(bf16[1,128,128]{1,2,0:T(8,128)(2,1)S(1)} %fusion.74), channel_id=1, source_target_pairs={{0,64},{64,128},{128,192},{192,256},{256,320},{320,384},{384,448},... | collective-permute-start | bytes 98312 | tf_op jit(solution)/shard_map/ppermute | solution.py:10
  204.4 23.7 %all_gather.25 = bf16[16,128,128]{2,1,0:T(8,128)(2,1)S(1)} all-gather(bf16[1,128,128]{2,1,0:T(8,128)(2,1)S(1)} %copy.42), channel_id=1, replica_groups=mesh['level'=8,'row'=16,'col'=4] {'row'}, dimensions={0}, use_global_device_ids=true | all-gather | bytes 557056 | tf_op jit(solution)/shard_map/all_gather | solution.py:45
  236.2 12.5 %collective-permute-start.5 = (bf16[1,128,128]{1,2,0:T(8,128)(2,1)S(1)}, bf16[1,128,128]{1,2,0:T(8,128)(2,1)S(1)}, u32[]{:S(2)}, u32[]{:S(2)}) collective-permute-start(bf16[1,128,128]{1,2,0:T(8,128)(2,1)S(1)} %fusion.75), channel_id=1, source_target_pairs={{0,64},{64,128},{128,192},{192,256},{256,320},{320,384},{384,448},... | collective-permute-start | bytes 98312 | tf_op jit(solution)/shard_map/ppermute | solution.py:10
  249.8 22.7 %all_gather.26 = bf16[16,128,128]{2,1,0:T(8,128)(2,1)S(1)} all-gather(bf16[1,128,128]{2,1,0:T(8,128)(2,1)S(1)} %copy.44), channel_id=1, replica_groups=mesh['level'=8,'row'=16,'col'=4] {'row'}, dimensions={0}, use_global_device_ids=true | all-gather | bytes 557056 | tf_op jit(solution)/shard_map/all_gather | solution.py:45
  280.8 12.4 %collective-permute-start.6 = (bf16[1,128,128]{1,2,0:T(8,128)(2,1)S(1)}, bf16[1,128,128]{1,2,0:T(8,128)(2,1)S(1)}, u32[]{:S(2)}, u32[]{:S(2)}) collective-permute-start(bf16[1,128,128]{1,2,0:T(8,128)(2,1)S(1)} %fusion.76), channel_id=1, source_target_pairs={{0,64},{64,128},{128,192},{192,256},{256,320},{320,384},{384,448},... | collective-permute-start | bytes 98312 | tf_op jit(solution)/shard_map/ppermute | solution.py:10
  294.2 23.5 %all_gather.27 = bf16[16,128,128]{2,1,0:T(8,128)(2,1)S(1)} all-gather(bf16[1,128,128]{2,1,0:T(8,128)(2,1)S(1)} %copy.46), channel_id=1, replica_groups=mesh['level'=8,'row'=16,'col'=4] {'row'}, dimensions={0}, use_global_device_ids=true | all-gather | bytes 557056 | tf_op jit(solution)/shard_map/all_gather | solution.py:45
  334.8 61.1 %reduce-scatter.8.cloned.1.call-done = bf16[1,128,128]{1,2,0:T(8,128)(2,1)} async-done(((bf16[16,128,128]{1,2,0:T(8,128)(2,1)}), bf16[1,128,128]{1,2,0:T(8,128)(2,1)}) %reduce-scatter.8.cloned.1.call-update) | async-done | bytes 32784 | tf_op jit(solution)/shard_map/reduce_scatter | solution.py:67
  395.9 14.1 %collective-permute-start.7 = (bf16[1,128,128]{1,2,0:T(8,128)(2,1)}, bf16[1,128,128]{1,2,0:T(8,128)(2,1)S(1)}, u32[]{:S(2)}, u32[]{:S(2)}) collective-permute-start(bf16[1,128,128]{1,2,0:T(8,128)(2,1)} %reduce-scatter.8.cloned.1.call-done), channel_id=1, source_target_pairs={{64,0},{128,64},{192,128},{256,192},{320,256},{384,320},{448,384},... | collective-permute-start | bytes 98312 | tf_op jit(solution)/shard_map/ppermute | solution.py:10
  423.2 54.6 %reduce-scatter.10.cloned.1.call-done = bf16[1,128,128]{1,2,0:T(8,128)(2,1)} async-done(((bf16[16,128,128]{1,2,0:T(8,128)(2,1)}), bf16[1,128,128]{1,2,0:T(8,128)(2,1)}) %reduce-scatter.10.cloned.1.call-update) | async-done | bytes 32784 | tf_op jit(solution)/shard_map/reduce_scatter | solution.py:67
  477.8 13.7 %collective-permute-start.8 = (bf16[1,128,128]{1,2,0:T(8,128)(2,1)}, bf16[1,128,128]{1,2,0:T(8,128)(2,1)S(1)}, u32[]{:S(2)}, u32[]{:S(2)}) collective-permute-start(bf16[1,128,128]{1,2,0:T(8,128)(2,1)} %reduce-scatter.10.cloned.1.call-done), channel_id=1, source_target_pairs={{64,0},{128,64},{192,128},{256,192},{320,256},{384,320},{448,384},... | collective-permute-start | bytes 98312 | tf_op jit(solution)/shard_map/ppermute | solution.py:10
  494.6 8.7 all_to_all.79
  504.6 55.2 %reduce-scatter.12.cloned.1.call-done = bf16[1,128,128]{1,2,0:T(8,128)(2,1)} async-done(((bf16[16,128,128]{1,2,0:T(8,128)(2,1)}), bf16[1,128,128]{1,2,0:T(8,128)(2,1)}) %reduce-scatter.12.cloned.1.call-update) | async-done | bytes 32784 | tf_op jit(solution)/shard_map/reduce_scatter | solution.py:67
  559.8 12.9 %collective-permute-start.9 = (bf16[1,128,128]{1,2,0:T(8,128)(2,1)}, bf16[1,128,128]{1,2,0:T(8,128)(2,1)S(1)}, u32[]{:S(2)}, u32[]{:S(2)}) collective-permute-start(bf16[1,128,128]{1,2,0:T(8,128)(2,1)} %reduce-scatter.12.cloned.1.call-done), channel_id=1, source_target_pairs={{64,0},{128,64},{192,128},{256,192},{320,256},{384,320},{448,384},... | collective-permute-start | bytes 98312 | tf_op jit(solution)/shard_map/ppermute | solution.py:10
  585.9 54.2 %reduce-scatter.14.cloned.1.call-done = bf16[1,128,128]{1,2,0:T(8,128)(2,1)} async-done(((bf16[16,128,128]{1,2,0:T(8,128)(2,1)}), bf16[1,128,128]{1,2,0:T(8,128)(2,1)}) %reduce-scatter.14.cloned.1.call-update) | async-done | bytes 32784 | tf_op jit(solution)/shard_map/reduce_scatter | solution.py:67
  640.1 13.9 %collective-permute-start.10 = (bf16[1,128,128]{1,2,0:T(8,128)(2,1)}, bf16[1,128,128]{1,2,0:T(8,128)(2,1)S(1)}, u32[]{:S(2)}, u32[]{:S(2)}) collective-permute-start(bf16[1,128,128]{1,2,0:T(8,128)(2,1)} %reduce-scatter.14.cloned.1.call-done), channel_id=1, source_target_pairs={{64,0},{128,64},{192,128},{256,192},{320,256},{384,320},{448,384},... | collective-permute-start | bytes 98312 | tf_op jit(solution)/shard_map/ppermute | solution.py:10
  657.1 8.7 all_to_all.81
  667.1 54.1 %reduce-scatter.16.cloned.1.call-done = bf16[1,128,128]{1,2,0:T(8,128)(2,1)} async-done(((bf16[16,128,128]{1,2,0:T(8,128)(2,1)}), bf16[1,128,128]{1,2,0:T(8,128)(2,1)}) %reduce-scatter.16.cloned.1.call-update) | async-done | bytes 32784 | tf_op jit(solution)/shard_map/reduce_scatter | solution.py:67
  721.3 13.9 %collective-permute-start.11 = (bf16[1,128,128]{1,2,0:T(8,128)(2,1)}, bf16[1,128,128]{1,2,0:T(8,128)(2,1)S(1)}, u32[]{:S(2)}, u32[]{:S(2)}) collective-permute-start(bf16[1,128,128]{1,2,0:T(8,128)(2,1)} %reduce-scatter.16.cloned.1.call-done), channel_id=1, source_target_pairs={{64,0},{128,64},{192,128},{256,192},{320,256},{384,320},{448,384},... | collective-permute-start | bytes 98312 | tf_op jit(solution)/shard_map/ppermute | solution.py:10
  738.3 8.7 all_to_all.82
  748.4 54.9 %reduce-scatter.18.cloned.1.call-done = bf16[1,128,128]{1,2,0:T(8,128)(2,1)} async-done(((bf16[16,128,128]{1,2,0:T(8,128)(2,1)}), bf16[1,128,128]{1,2,0:T(8,128)(2,1)}) %reduce-scatter.18.cloned.1.call-update) | async-done | bytes 32784 | tf_op jit(solution)/shard_map/reduce_scatter | solution.py:67
  803.3 13.2 %collective-permute-start.12 = (bf16[1,128,128]{1,2,0:T(8,128)(2,1)}, bf16[1,128,128]{1,2,0:T(8,128)(2,1)S(1)}, u32[]{:S(2)}, u32[]{:S(2)}) collective-permute-start(bf16[1,128,128]{1,2,0:T(8,128)(2,1)} %reduce-scatter.18.cloned.1.call-done), channel_id=1, source_target_pairs={{64,0},{128,64},{192,128},{256,192},{320,256},{384,320},{448,384},... | collective-permute-start | bytes 98312 | tf_op jit(solution)/shard_map/ppermute | solution.py:10
  819.7 8.7 all_to_all.83
  829.7 54.6 %reduce-scatter.20.cloned.1.call-done = bf16[1,128,128]{1,2,0:T(8,128)(2,1)} async-done(((bf16[16,128,128]{1,2,0:T(8,128)(2,1)}), bf16[1,128,128]{1,2,0:T(8,128)(2,1)}) %reduce-scatter.20.cloned.1.call-update) | async-done | bytes 32784 | tf_op jit(solution)/shard_map/reduce_scatter | solution.py:67
  884.3 13.6 %collective-permute-start.13 = (bf16[1,128,128]{1,2,0:T(8,128)(2,1)}, bf16[1,128,128]{1,2,0:T(8,128)(2,1)S(1)}, u32[]{:S(2)}, u32[]{:S(2)}) collective-permute-start(bf16[1,128,128]{1,2,0:T(8,128)(2,1)} %reduce-scatter.20.cloned.1.call-done), channel_id=1, source_target_pairs={{64,0},{128,64},{192,128},{256,192},{320,256},{384,320},{448,384},... | collective-permute-start | bytes 98312 | tf_op jit(solution)/shard_map/ppermute | solution.py:10
  (105 shorter events, 126.6 us)
Async XLA Ops:
  7.2 0.8 copy-start
  7.2 388.7 %reduce-scatter.8.cloned.1.call-start = ((), (), s32[]{:S(2)}) async-start(), calls=%async_computation.21 | async-start | bytes 557056 | tf_op jit(solution)/shard_map/reduce_scatter | solution.py:67
  8.9 8.9 collective-permute-start
  46.3 11.3 %copy-start.1 = (f32[1,1,1,128,128]{4,3,2,1,0:T(8,128)S(1)}, f32[1,1,1,128,128]{4,3,2,1,0:T(8,128)}, u32[]{:S(2)}) copy-start(f32[1,1,1,128,128]{4,3,2,1,0:T(8,128)} %param.7) | copy-start | bytes 196612
  46.3 47.4 %copy-start.2 = (bf16[1,4,16,1,128,128]{5,4,3,2,1,0:T(8,128)(2,1)S(1)}, bf16[1,4,16,1,128,128]{5,4,3,2,1,0:T(8,128)(2,1)}, u32[]{:S(2)}) copy-start(bf16[1,4,16,1,128,128]{5,4,3,2,1,0:T(8,128)(2,1)} %param.4) | copy-start | bytes 6291460
  57.9 13.0 %collective-permute-start.1 = (bf16[1,128,128]{1,2,0:T(8,128)(2,1)S(1)}, bf16[1,128,128]{1,2,0:T(8,128)(2,1)S(1)}, u32[]{:S(2)}, u32[]{:S(2)}) collective-permute-start(bf16[1,128,128]{1,2,0:T(8,128)(2,1)S(1)} %fusion.71), channel_id=1, source_target_pairs={{0,64},{64,128},{128,192},{192,256},{256,320},{320,384},{384,448},... | collective-permute-start | bytes 98312 | tf_op jit(solution)/shard_map/ppermute | solution.py:10
  101.9 13.0 %collective-permute-start.2 = (bf16[1,128,128]{1,2,0:T(8,128)(2,1)S(1)}, bf16[1,128,128]{1,2,0:T(8,128)(2,1)S(1)}, u32[]{:S(2)}, u32[]{:S(2)}) collective-permute-start(bf16[1,128,128]{1,2,0:T(8,128)(2,1)S(1)} %fusion.72), channel_id=1, source_target_pairs={{0,64},{64,128},{128,192},{192,256},{256,320},{320,384},{384,448},... | collective-permute-start | bytes 98312 | tf_op jit(solution)/shard_map/ppermute | solution.py:10
  147.9 12.6 %collective-permute-start.3 = (bf16[1,128,128]{1,2,0:T(8,128)(2,1)S(1)}, bf16[1,128,128]{1,2,0:T(8,128)(2,1)S(1)}, u32[]{:S(2)}, u32[]{:S(2)}) collective-permute-start(bf16[1,128,128]{1,2,0:T(8,128)(2,1)S(1)} %fusion.73), channel_id=1, source_target_pairs={{0,64},{64,128},{128,192},{192,256},{256,320},{320,384},{384,448},... | collective-permute-start | bytes 98312 | tf_op jit(solution)/shard_map/ppermute | solution.py:10
  191.6 12.7 %collective-permute-start.4 = (bf16[1,128,128]{1,2,0:T(8,128)(2,1)S(1)}, bf16[1,128,128]{1,2,0:T(8,128)(2,1)S(1)}, u32[]{:S(2)}, u32[]{:S(2)}) collective-permute-start(bf16[1,128,128]{1,2,0:T(8,128)(2,1)S(1)} %fusion.74), channel_id=1, source_target_pairs={{0,64},{64,128},{128,192},{192,256},{256,320},{320,384},{384,448},... | collective-permute-start | bytes 98312 | tf_op jit(solution)/shard_map/ppermute | solution.py:10
  236.2 13.5 %collective-permute-start.5 = (bf16[1,128,128]{1,2,0:T(8,128)(2,1)S(1)}, bf16[1,128,128]{1,2,0:T(8,128)(2,1)S(1)}, u32[]{:S(2)}, u32[]{:S(2)}) collective-permute-start(bf16[1,128,128]{1,2,0:T(8,128)(2,1)S(1)} %fusion.75), channel_id=1, source_target_pairs={{0,64},{64,128},{128,192},{192,256},{256,320},{320,384},{384,448},... | collective-permute-start | bytes 98312 | tf_op jit(solution)/shard_map/ppermute | solution.py:10
  280.8 13.4 %collective-permute-start.6 = (bf16[1,128,128]{1,2,0:T(8,128)(2,1)S(1)}, bf16[1,128,128]{1,2,0:T(8,128)(2,1)S(1)}, u32[]{:S(2)}, u32[]{:S(2)}) collective-permute-start(bf16[1,128,128]{1,2,0:T(8,128)(2,1)S(1)} %fusion.76), channel_id=1, source_target_pairs={{0,64},{64,128},{128,192},{192,256},{256,320},{320,384},{384,448},... | collective-permute-start | bytes 98312 | tf_op jit(solution)/shard_map/ppermute | solution.py:10
  334.8 143.0 %reduce-scatter.10.cloned.1.call-start = ((), (), s32[]{:S(2)}) async-start(), calls=%async_computation.22 | async-start | bytes 557056 | tf_op jit(solution)/shard_map/reduce_scatter | solution.py:67
  395.9 16.9 %collective-permute-start.7 = (bf16[1,128,128]{1,2,0:T(8,128)(2,1)}, bf16[1,128,128]{1,2,0:T(8,128)(2,1)S(1)}, u32[]{:S(2)}, u32[]{:S(2)}) collective-permute-start(bf16[1,128,128]{1,2,0:T(8,128)(2,1)} %reduce-scatter.8.cloned.1.call-done), channel_id=1, source_target_pairs={{64,0},{128,64},{192,128},{256,192},{320,256},{384,320},{448,384},... | collective-permute-start | bytes 98312 | tf_op jit(solution)/shard_map/ppermute | solution.py:10
  423.1 136.7 %reduce-scatter.12.cloned.1.call-start = ((), (), s32[]{:S(2)}) async-start(), calls=%async_computation.23 | async-start | bytes 557056 | tf_op jit(solution)/shard_map/reduce_scatter | solution.py:67
  477.8 16.5 %collective-permute-start.8 = (bf16[1,128,128]{1,2,0:T(8,128)(2,1)}, bf16[1,128,128]{1,2,0:T(8,128)(2,1)S(1)}, u32[]{:S(2)}, u32[]{:S(2)}) collective-permute-start(bf16[1,128,128]{1,2,0:T(8,128)(2,1)} %reduce-scatter.10.cloned.1.call-done), channel_id=1, source_target_pairs={{64,0},{128,64},{192,128},{256,192},{320,256},{384,320},{448,384},... | collective-permute-start | bytes 98312 | tf_op jit(solution)/shard_map/ppermute | solution.py:10
  504.6 135.5 %reduce-scatter.14.cloned.1.call-start = ((), (), s32[]{:S(2)}) async-start(), calls=%async_computation.24 | async-start | bytes 557056 | tf_op jit(solution)/shard_map/reduce_scatter | solution.py:67
  559.8 15.8 %collective-permute-start.9 = (bf16[1,128,128]{1,2,0:T(8,128)(2,1)}, bf16[1,128,128]{1,2,0:T(8,128)(2,1)S(1)}, u32[]{:S(2)}, u32[]{:S(2)}) collective-permute-start(bf16[1,128,128]{1,2,0:T(8,128)(2,1)} %reduce-scatter.12.cloned.1.call-done), channel_id=1, source_target_pairs={{64,0},{128,64},{192,128},{256,192},{320,256},{384,320},{448,384},... | collective-permute-start | bytes 98312 | tf_op jit(solution)/shard_map/ppermute | solution.py:10
  585.9 135.4 %reduce-scatter.16.cloned.1.call-start = ((), (), s32[]{:S(2)}) async-start(), calls=%async_computation.25 | async-start | bytes 557056 | tf_op jit(solution)/shard_map/reduce_scatter | solution.py:67
  640.1 16.7 %collective-permute-start.10 = (bf16[1,128,128]{1,2,0:T(8,128)(2,1)}, bf16[1,128,128]{1,2,0:T(8,128)(2,1)S(1)}, u32[]{:S(2)}, u32[]{:S(2)}) collective-permute-start(bf16[1,128,128]{1,2,0:T(8,128)(2,1)} %reduce-scatter.14.cloned.1.call-done), channel_id=1, source_target_pairs={{64,0},{128,64},{192,128},{256,192},{320,256},{384,320},{448,384},... | collective-permute-start | bytes 98312 | tf_op jit(solution)/shard_map/ppermute | solution.py:10
  667.1 136.2 %reduce-scatter.18.cloned.1.call-start = ((), (), s32[]{:S(2)}) async-start(), calls=%async_computation.26 | async-start | bytes 557056 | tf_op jit(solution)/shard_map/reduce_scatter | solution.py:67
  721.3 16.7 %collective-permute-start.11 = (bf16[1,128,128]{1,2,0:T(8,128)(2,1)}, bf16[1,128,128]{1,2,0:T(8,128)(2,1)S(1)}, u32[]{:S(2)}, u32[]{:S(2)}) collective-permute-start(bf16[1,128,128]{1,2,0:T(8,128)(2,1)} %reduce-scatter.16.cloned.1.call-done), channel_id=1, source_target_pairs={{64,0},{128,64},{192,128},{256,192},{320,256},{384,320},{448,384},... | collective-permute-start | bytes 98312 | tf_op jit(solution)/shard_map/ppermute | solution.py:10
  748.3 136.0 %reduce-scatter.20.cloned.1.call-start = ((), (), s32[]{:S(2)}) async-start(), calls=%async_computation.27 | async-start | bytes 557056 | tf_op jit(solution)/shard_map/reduce_scatter | solution.py:67
  803.3 16.1 %collective-permute-start.12 = (bf16[1,128,128]{1,2,0:T(8,128)(2,1)}, bf16[1,128,128]{1,2,0:T(8,128)(2,1)S(1)}, u32[]{:S(2)}, u32[]{:S(2)}) collective-permute-start(bf16[1,128,128]{1,2,0:T(8,128)(2,1)} %reduce-scatter.18.cloned.1.call-done), channel_id=1, source_target_pairs={{64,0},{128,64},{192,128},{256,192},{320,256},{384,320},{448,384},... | collective-permute-start | bytes 98312 | tf_op jit(solution)/shard_map/ppermute | solution.py:10
  884.3 16.5 %collective-permute-start.13 = (bf16[1,128,128]{1,2,0:T(8,128)(2,1)}, bf16[1,128,128]{1,2,0:T(8,128)(2,1)S(1)}, u32[]{:S(2)}, u32[]{:S(2)}) collective-permute-start(bf16[1,128,128]{1,2,0:T(8,128)(2,1)} %reduce-scatter.20.cloned.1.call-done), channel_id=1, source_target_pairs={{64,0},{128,64},{192,128},{256,192},{320,256},{384,320},{448,384},... | collective-permute-start | bytes 98312 | tf_op jit(solution)/shard_map/ppermute | solution.py:10
Sparse Core Ops, SparseCore 0:
  334.9 60.9 reduce-scatter.7
  423.2 54.4 reduce-scatter.9
  504.7 55.0 reduce-scatter.11
  586.0 54.0 reduce-scatter.13
  667.2 54.0 reduce-scatter.15
  748.4 54.8 reduce-scatter.17
  829.8 54.4 reduce-scatter.19
